TPU v7x, 256 devices: a whole 4x4x8 slice. The times are simulated.
256 devices in a mesh: grp: 8 (over z), seq: 32 (over y, x, core).
Axes of the slice: x: 4, y: 4, z: 8, core: 2. Of those that a mesh axis runs over, the one named last changes fastest.
Arguments:
- queries: bfloat16 [28, 4096, 2048], P(None, ('grp', 'seq')), parts along dimension 1, may hold values from -16 to 16
- keys: bfloat16 [28, 4096, 2048], P(None, ('grp', 'seq')), parts along dimension 1, may hold values from -16 to 16
- values: bfloat16 [28, 4096, 2048], P(None, ('grp', 'seq')), parts along dimension 1, may hold values from -6 to 6
- cotangent: bfloat16 [28, 4096, 2048], P(None, ('grp', 'seq')), parts along dimension 1, may hold values from -6 to 6
- lengths: int32 [384], P('grp'), parts along dimension 0, may hold values from 16 to 512, as said below
Outputs:
- grad_queries: bfloat16 [28, 4096, 2048], P(None, ('grp', 'seq')), parts along dimension 1
- grad_keys: bfloat16 [28, 4096, 2048], P(None, ('grp', 'seq')), parts along dimension 1
- grad_values: bfloat16 [28, 4096, 2048], P(None, ('grp', 'seq')), parts along dimension 1
There are 8 independent parts, one for each index of `grp`. A program takes and returns all parts, laid end to end along the dimension named above; each array names one. Nothing has to cross between parts.
Inputs may be any that keep to these rules, and one draw needn't show every extreme that they name: Every length is a multiple of 16; the lengths sum to 14336.
All inputs are finite; a program needn't handle non-finite values.
Results may differ from a plain program's by a relative error of at most 0.0093.
Values may be sent and summed in bfloat16 or wider, within the bound.
A program may use at most 192 MiB of HBM per device.

v0:
```python
import math

import jax
import jax.numpy as jnp
from jax import lax
from jax.sharding import PartitionSpec as P

HEADS = 16
HEAD_DIM = 128
SLOTS = 2


def lookup(table, wanted):
    positions = jnp.arange(table.shape[0], dtype=jnp.int32)
    hits = wanted[..., None] == positions
    return jnp.sum(jnp.where(hits, table, 0), axis=-1)


def head_grads(blocks, allowed):
    query_rows = blocks[0]
    key_rows = blocks[1]
    value_rows = blocks[2]
    cot_rows = blocks[3]
    score_scale = 1.0 / math.sqrt(query_rows.shape[-1])
    scores = jnp.dot(query_rows, key_rows.T, preferred_element_type=jnp.float32) * score_scale
    scores = jnp.where(allowed, scores, -1e30)
    row_max = jnp.max(scores, axis=1, keepdims=True)
    weights = jnp.where(allowed, jnp.exp(scores - row_max), 0.0)
    denominator = jnp.sum(weights, axis=1, keepdims=True)
    denominator = jnp.where(denominator > 0.0, denominator, 1.0)
    probs = weights / denominator
    probs_low = probs.astype(jnp.bfloat16)
    grad_probs = jnp.dot(cot_rows, value_rows.T, preferred_element_type=jnp.float32)
    output = jnp.dot(probs_low, value_rows, preferred_element_type=jnp.float32)
    row_delta = jnp.sum(cot_rows.astype(jnp.float32) * output, axis=1, keepdims=True)
    grad_scores = (probs * (grad_probs - row_delta)).astype(jnp.bfloat16)
    grad_query = jnp.dot(grad_scores, key_rows, preferred_element_type=jnp.float32) * score_scale
    grad_key = jnp.dot(grad_scores.T, query_rows, preferred_element_type=jnp.float32) * score_scale
    grad_value = jnp.dot(probs_low.T, cot_rows, preferred_element_type=jnp.float32)
    return jnp.stack([grad_query, grad_key, grad_value]).astype(jnp.bfloat16)


def slot_grads(window, valid):
    band_rows = window.shape[0]
    full_width = window.shape[-1]
    allowed = valid[:, None] & valid[None, :]
    per_head = window.reshape(band_rows, 4, HEADS, HEAD_DIM).transpose(2, 1, 0, 3)
    result = lax.map(lambda blocks: head_grads(blocks, allowed), per_head)
    result = result.transpose(2, 1, 0, 3).reshape(band_rows, 3, full_width)
    return jnp.where(valid[:, None, None], result, jnp.zeros((), jnp.bfloat16))


def owner_work(pieces):
    rows_in = pieces[0]
    present_in = pieces[1]
    item_count, peer_count, tile_rows = present_in.shape
    band_rows = peer_count * tile_rows
    full_width = rows_in.shape[-1]
    rows_in = rows_in.reshape(item_count, band_rows, 4, full_width)
    valid_rows = present_in.reshape(item_count, band_rows) > 0.5
    gradients = lax.map(lambda member: slot_grads(member[0], member[1]), (rows_in, valid_rows))
    return gradients.reshape(item_count, peer_count, tile_rows, 3, full_width)


def assign_owners(tile_lengths, devices):
    doc_count = tile_lengths.shape[0]
    doc_index = jnp.arange(doc_count, dtype=jnp.int32)
    doc_cost = tile_lengths * tile_lengths
    ranking = jnp.argsort(doc_index - doc_cost * doc_count, stable=True)
    owner_ids = jnp.arange(devices, dtype=jnp.int32)

    def place(placed, placing):
        owner_loads, filled, owner_of, slot_of = placing
        current = lookup(ranking, placed)
        ranking_score = jnp.where(filled < SLOTS, owner_loads * devices + owner_ids, 2**30)
        chosen = jnp.argmin(ranking_score)
        picked = owner_ids == chosen
        slot_now = jnp.sum(jnp.where(picked, filled, 0))
        owner_loads = owner_loads + jnp.where(picked, lookup(doc_cost, current), 0)
        filled = filled + picked.astype(jnp.int32)
        is_doc = doc_index == current
        owner_of = jnp.where(is_doc, chosen, owner_of)
        slot_of = jnp.where(is_doc, slot_now, slot_of)
        return (owner_loads, filled, owner_of, slot_of)

    owner_zeros = jnp.zeros((devices,), jnp.int32)
    doc_zeros = jnp.zeros((doc_count,), jnp.int32)
    placing = lax.fori_loop(0, doc_count, place, (owner_zeros, owner_zeros, doc_zeros, doc_zeros))
    owner_of = placing[2]
    slot_of = placing[3]
    flat_slot = slot_of * devices + owner_of
    slot_index = jnp.arange(SLOTS * devices, dtype=jnp.int32)
    matches = flat_slot[None, :] == slot_index[:, None]
    owned_docs = jnp.where(
        jnp.any(matches, axis=1), jnp.sum(jnp.where(matches, doc_index, 0), axis=1), -1
    )
    return (owner_of, slot_of, owned_docs.reshape(SLOTS, devices))


def per_device(queries, keys, values, cotangent, lengths):
    rounds, tile_rows, full_width = queries.shape
    devices = lax.axis_size("seq")
    device_index = lax.axis_index("seq")
    tile_lengths = lengths // tile_rows
    tile_starts = jnp.cumsum(tile_lengths) - tile_lengths
    owner_of, slot_of, owned_docs = assign_owners(tile_lengths, devices)
    holder = jnp.maximum(owned_docs, 0)
    begin_tile = lookup(tile_starts, holder)
    span_tiles = lookup(tile_lengths, holder)
    offset_tiles = jnp.mod(device_index - begin_tile, devices)
    touches = (owned_docs >= 0) & (offset_tiles < span_tiles)
    round_of = jnp.clip((begin_tile + offset_tiles) // devices, 0, rounds - 1)
    local_rows = jnp.stack([queries, keys, values, cotangent], axis=2)
    outgoing = jnp.where(
        touches[:, :, None, None, None], local_rows[round_of], jnp.zeros((), jnp.bfloat16)
    )
    present = jnp.broadcast_to(touches[:, :, None], touches.shape + (tile_rows,)).astype(
        jnp.bfloat16
    )
    computed = owner_work(
        (
            lax.all_to_all(outgoing, "seq", split_axis=1, concat_axis=1, tiled=True),
            lax.all_to_all(present, "seq", split_axis=1, concat_axis=1, tiled=True),
        )
    )
    homeward = lax.all_to_all(computed, "seq", split_axis=1, concat_axis=1, tiled=True)
    tile_ids = jnp.arange(rounds, dtype=jnp.int32) * devices + device_index
    doc_of_tile = jnp.sum(tile_ids[:, None] >= tile_starts[None, :], axis=1) - 1
    home_owner = lookup(owner_of, doc_of_tile)
    home_slot = lookup(slot_of, doc_of_tile)
    flat_home = homeward.reshape(SLOTS * devices, tile_rows, 3, full_width)
    gathered = flat_home[home_slot * devices + home_owner]
    return (gathered[:, :, 0], gathered[:, :, 1], gathered[:, :, 2])


def solution(mesh):
    placed = (
        P(None, ("grp", "seq"), None),
        P(None, ("grp", "seq"), None),
        P(None, ("grp", "seq"), None),
        P(None, ("grp", "seq"), None),
        P("grp"),
    )
    return jax.shard_map(
        per_device,
        mesh=mesh,
        in_specs=placed,
        out_specs=(
            P(None, ("grp", "seq"), None),
            P(None, ("grp", "seq"), None),
            P(None, ("grp", "seq"), None),
        ),
        check_vma=False,
    )
```

profile of v0, /device:TPU:1, one launch (start us, length us, event | category | flops | bytes accessed | tf_op | source)
XLA Modules:
  0.0 1044.2 jit_solution(5829531177364134848)
XLA Ops:
  1.6 2.0 sort.17
  3.7 342.8 %while.44 = (s32[]{:T(128)}, s32[32]{0:T(128)S(1)}, s32[32]{0:T(128)S(1)}, s32[48]{0:T(128)S(1)}, s32[48]{0:T(128)S(1)}, /*index=5*/s32[48]{0:T(128)S(1)}, s32[48]{0:T(128)S(1)}, s32[]{:T(128)}, s32[]{:T(128)}) while((s32[]{:T(128)}, s32[32]{0:T(128)S(1)}, s32[32]{0:T(128)S(1)}, s32[48]{0:T(128)S(1)}, s32[48]{0:T(128)S(1)}, ...), condition=%wide.region_6.7_spmd.clone.clone, body=%wide.region_1.0_spmd.clone.clone.sunk | while | flops 1257 | bytes 2078 | solution.py:88
  6.4 1.9 compare_select_fusion.17
  20.7 1.9 compare_select_fusion.17
  27.8 1.9 compare_select_fusion.17
  348.0 8.6 all-to-all-start
  356.7 6.7 pad_maximum_fusion.1
  363.4 10.6 %gather_fusion = bf16[64,16,4,2048]{3,1,2,0:T(8,128)(2,1)} fusion(bf16[28,16,4,2048]{3,1,0,2:T(8,128)(2,1)} %pad_maximum_fusion.1, s32[1024]{0:T(1024)S(1)} %pad_clamp_fusion.1), kind=kCustom, calls=%fused_computation | custom fusion | bytes 33554688 | tf_op jit(solution)/shard_map/gather | solution.py:115
  374.0 8.3 broadcast_select_fusion.4
  382.3 6.6 copy.64
  388.9 7.4 all-to-all-start.1
  396.6 201.6 %all-to-all-done.1 = bf16[2,32,16,4,2048]{4,2,3,0,1:T(8,128)(2,1)} async-done(((bf16[2,32,16,4,2048]{4,2,3,0,1:T(8,128)(2,1)}), bf16[2,32,16,4,2048]{4,2,3,0,1:T(8,128)(2,1)}, u32[]{:S(2)}, u32[]{:S(2)}) %all-to-all-start.1) | async-done | bytes 16777248 | tf_op jit(solution)/shard_map/all_to_all | solution.py:122
  598.3 14.1 %copy.65 = bf16[2,32,16,4,2048]{4,2,1,3,0:T(8,128)(2,1)} copy(bf16[2,32,16,4,2048]{4,2,3,0,1:T(8,128)(2,1)} %all-to-all-done.1) | data formatting | bytes 33554432 | tf_op jit(solution)/shard_map/all_to_all | solution.py:122
  612.4 229.1 %while.43 = (s32[]{:T(128)}, bf16[2,512,3,2048]{3,1,2,0:T(8,128)(2,1)}, pred[2,512]{1,0:T(4,128)(4,1)S(1)}, bf16[2,512,4,2048]{3,1,2,0:T(8,128)(2,1)}, s32[]{:T(128)}, /*index=5*/s32[]{:T(128)}, s32[]{:T(128)}) while((s32[]{:T(128)}, bf16[2,512,3,2048]{3,1,2,0:T(8,128)(2,1)}, pred[2,512]{1,0:T(4,128)(4,1)S(1)}, ...), condition=%wide.region_18.19_spmd, body=%wide.region_12.18_spmd.sunk | while | flops 411172352 | bytes 85220032 | solution.py:61
  612.4 8.3 constant_dynamic-slice_fusion.2
  620.7 11.4 %copy.80 = bf16[1,512,4,2048]{1,3,2,0:T(8,128)(2,1)} copy(bf16[1,512,4,2048]{3,1,2,0:T(8,128)(2,1)} %constant_dynamic-slice_fusion.2) | data formatting | bytes 16777216 | tf_op jit(solution)/shard_map/while/body/jit(dynamic_index_in_dim)/dynamic_slice | solution.py:61
  632.1 73.8 %while.45 = (s32[]{:T(128)}, bf16[16,3,512,128]{2,3,0,1:T(8,128)(2,1)}, bf16[16,4,512,128]{2,3,0,1:T(8,128)(2,1)}, pred[512]{0:T(512)(128)(4,1)S(1)}, s32[]{:T(128)}) while((s32[]{:T(128)}, bf16[16,3,512,128]{2,3,0,1:T(8,128)(2,1)}, bf16[16,4,512,128]{2,3,0,1:T(8,128)(2,1)}, pred[512]{0:T(512)(128)(4,1)S(1)}, s32[]{:T(128)}) %tuple.109), condition=%wide.region_17.17_spmd.clone, body=%wide.region_13.16_spmd.clone.sunk | while | flops 408026624 | bytes 13914689 | solution.py:48
  705.8 5.8 bitcast_select_fusion.2
  711.6 8.8 copy.81
  720.5 6.5 constant_dynamic-update-slice_fusion.4
  727.0 8.3 constant_dynamic-slice_fusion.2
  735.3 11.4 %copy.80 = bf16[1,512,4,2048]{1,3,2,0:T(8,128)(2,1)} copy(bf16[1,512,4,2048]{3,1,2,0:T(8,128)(2,1)} %constant_dynamic-slice_fusion.2) | data formatting | bytes 16777216 | tf_op jit(solution)/shard_map/while/body/jit(dynamic_index_in_dim)/dynamic_slice | solution.py:61
  746.6 73.8 %while.45 = (s32[]{:T(128)}, bf16[16,3,512,128]{2,3,0,1:T(8,128)(2,1)}, bf16[16,4,512,128]{2,3,0,1:T(8,128)(2,1)}, pred[512]{0:T(512)(128)(4,1)S(1)}, s32[]{:T(128)}) while((s32[]{:T(128)}, bf16[16,3,512,128]{2,3,0,1:T(8,128)(2,1)}, bf16[16,4,512,128]{2,3,0,1:T(8,128)(2,1)}, pred[512]{0:T(512)(128)(4,1)S(1)}, s32[]{:T(128)}) %tuple.109), condition=%wide.region_17.17_spmd.clone, body=%wide.region_13.16_spmd.clone.sunk | while | flops 408026624 | bytes 13914689 | solution.py:48
  820.4 5.8 bitcast_select_fusion.2
  826.2 8.8 copy.81
  835.0 6.5 constant_dynamic-update-slice_fusion.4
  841.6 10.8 %copy.68 = bf16[2,32,16,3,2048]{4,2,3,0,1:T(8,128)(2,1)} copy(bf16[2,32,16,3,2048]{4,2,1,3,0:T(8,128)(2,1)} %bitcast.107) | data formatting | bytes 25165824 | tf_op jit(solution)/shard_map/reshape | solution.py:62
  852.4 16.3 %all-to-all-start.2 = ((bf16[2,32,16,3,2048]{4,2,3,0,1:T(8,128)(2,1)}), bf16[2,32,16,3,2048]{4,2,3,0,1:T(8,128)(2,1)}, u32[]{:S(2)}, u32[]{:S(2)}) async-start(bf16[2,32,16,3,2048]{4,2,3,0,1:T(8,128)(2,1)} %copy.68), calls=%async_computation.2 | async-start | bytes 25165824 | tf_op jit(solution)/shard_map/all_to_all | solution.py:126
  869.1 151.0 %all-to-all-done.2 = bf16[2,32,16,3,2048]{4,2,3,0,1:T(8,128)(2,1)} async-done(((bf16[2,32,16,3,2048]{4,2,3,0,1:T(8,128)(2,1)}), bf16[2,32,16,3,2048]{4,2,3,0,1:T(8,128)(2,1)}, u32[]{:S(2)}, u32[]{:S(2)}) %all-to-all-start.2) | async-done | bytes 12582944 | tf_op jit(solution)/shard_map/all_to_all | solution.py:126
  1020.2 10.8 %copy.69 = bf16[2,32,16,3,2048]{4,2,3,1,0:T(8,128)(2,1)} copy(bf16[2,32,16,3,2048]{4,2,3,0,1:T(8,128)(2,1)} %all-to-all-done.2) | data formatting | bytes 25165824 | tf_op jit(solution)/shard_map/all_to_all | solution.py:126
  1031.0 7.9 gather_fusion.1
  1038.9 5.3 slice_bitcast_fusion.12
  (753 shorter events, 484.7 us)
Async XLA Ops:
  1.6 345.5 %copy-start.4 = (s32[48]{0:T(128)}, s32[48]{0:T(128)S(1)}, u32[]{:S(2)}) copy-start(s32[48]{0:T(128)S(1)} %get-tuple-element.365) | copy-start | bytes 580
  346.5 16.9 %copy-start = (s32[48]{0:T(128)}, s32[48]{0:T(128)S(1)}, u32[]{:S(2)}) copy-start(s32[48]{0:T(128)S(1)} %get-tuple-element.209) | copy-start | bytes 580
  346.5 16.8 %copy-start.2 = (s32[48]{0:T(128)}, s32[48]{0:T(128)S(1)}, u32[]{:S(2)}) copy-start(s32[48]{0:T(128)S(1)} %get-tuple-element.208) | copy-start | bytes 580
  348.0 40.9 %all-to-all-start = ((bf16[2,32,16]{2,0,1:T(2,128)(2,1)}), bf16[2,32,16]{2,0,1:T(2,128)(2,1)S(1)}, u32[]{:S(2)}, u32[]{:S(2)}) async-start(bf16[2,32,16]{2,0,1:T(2,128)(2,1)} %broadcast_in_dim.179), calls=%async_computation | async-start | bytes 32768 | tf_op jit(solution)/shard_map/all_to_all | solution.py:123
  388.9 209.4 %all-to-all-start.1 = ((bf16[2,32,16,4,2048]{4,2,3,0,1:T(8,128)(2,1)}), bf16[2,32,16,4,2048]{4,2,3,0,1:T(8,128)(2,1)}, u32[]{:S(2)}, u32[]{:S(2)}) async-start(bf16[2,32,16,4,2048]{4,2,3,0,1:T(8,128)(2,1)} %copy.64), calls=%async_computation.1 | async-start | bytes 33554432 | tf_op jit(solution)/shard_map/all_to_all | solution.py:122
  852.3 16.4 %copy-start.5 = (s32[48]{0:T(128)S(1)}, s32[48]{0:T(128)}, u32[]{:S(2)}) copy-start(s32[48]{0:T(128)} %copy-done.4) | copy-start | bytes 580
  852.3 16.6 %copy-start.1 = (s32[48]{0:T(128)S(1)}, s32[48]{0:T(128)}, u32[]{:S(2)}) copy-start(s32[48]{0:T(128)} %copy-done) | copy-start | bytes 580
  852.3 16.6 %copy-start.3 = (s32[48]{0:T(128)S(1)}, s32[48]{0:T(128)}, u32[]{:S(2)}) copy-start(s32[48]{0:T(128)} %copy-done.2) | copy-start | bytes 580
  852.4 167.8 %all-to-all-start.2 = ((bf16[2,32,16,3,2048]{4,2,3,0,1:T(8,128)(2,1)}), bf16[2,32,16,3,2048]{4,2,3,0,1:T(8,128)(2,1)}, u32[]{:S(2)}, u32[]{:S(2)}) async-start(bf16[2,32,16,3,2048]{4,2,3,0,1:T(8,128)(2,1)} %copy.68), calls=%async_computation.2 | async-start | bytes 25165824 | tf_op jit(solution)/shard_map/all_to_all | solution.py:126
where the time goes:
time: 1060 us; the launch traced here: 1040 us
  other arithmetic  391 us (37%)
  waiting for transfers between devices  353 us (33%)
  local copies, waits for them, and re-layouts  203 us (19%)
  matrix products  61.6 us (6%)
  starting transfers between devices  32.3 us (3%)
    all_to_all x1, waiting for transfers between devices, per_device(): lax.all_to_all(outgoing, 'seq', split_axis=1, concat_axis=1, tiled=True)  202 us
    all_to_all x1, waiting for transfers between devices, per_device(): lax.all_to_all(computed, 'seq', split_axis=1, concat_axis=1, tiled=True)  151 us
    reduce_sum x98, other arithmetic, lookup(): return jnp.sum(jnp.where(hits, table, 0), axis=-1)  91.7 us
    select_n x48, other arithmetic, place(): slot_of = jnp.where(is_doc, slot_now, slot_of)  91.3 us
    reduce_sum x48, other arithmetic, place(): slot_now = jnp.sum(jnp.where(picked, filled, 0))  63.5 us
    add x48, other arithmetic, place(): owner_loads = owner_loads + jnp.where(picked, lookup(doc_cost, current), 0)  60.3 us
    dynamic_slice x6, local copies, waits for them, and re-layouts, owner_work(): lax.map(lambda member: slot_grads(member[0], member[1]), (rows_in, valid_...  39.3 us
    another operation x48, other arithmetic, place(): chosen = jnp.argmin(ranking_score)  35.3 us
  transfers between devices with their start and end apart: 3, of which 2 were waited for; matrix products, arithmetic and copies ran while one was open for 3% of the time, Pallas kernels for 0%

commit v1 on v0

v1 whole, which is shorter than its diff:
```python
import functools
import math

import jax
import jax.numpy as jnp
from jax import lax
from jax.experimental import pallas as pl
from jax.experimental.pallas import tpu as pltpu
from jax.sharding import PartitionSpec as P

HEAD_DIM = 128
TILE = 16
SUB = 256
FAR = -1e30
MESH = pl.DeviceIdType.MESH
STEPS = (
    (1, 0), (0, 1), (3, 0), (0, 3), (1, 1), (3, 3), (2, 0), (0, 2),
    (1, 3), (3, 1), (2, 2), (2, 1), (1, 2), (2, 3), (3, 2), (0, 0),
)
PEERS = tuple((dx, dy, dc) for dx, dy in STEPS for dc in (0, 1) if (dx, dy, dc) != (0, 0, 0))
PIECE = 2
PIECES = 7
HALF = PIECE * PIECES
SLOTS = HALF + 1
SUBS = 2 * SLOTS
WINDOW = 5


def first_round(core, piece):
    return core * (HALF + PIECE * piece) + (1 - core) * (HALF - PIECE - PIECE * piece)


def first_slot(core, piece):
    return first_round(core, piece) - core * (HALF - 1)


def kernel(
    queries, keys, values, cotangent, lens,
    grad_queries, grad_keys, grad_values,
    held, apart, member, sum_keys, sum_values, staged,
    in_sent, in_came, halo_sent, halo_came, out_sent, out_came,
):
    me = lax.axis_index("seq")
    chip_y, chip_x, core = me // 8, lax.rem(me // 2, 4), lax.rem(me, 2)
    chip = me // 2
    other = chip * 2 + 1 - core
    sources = (queries, keys, values, cotangent)
    results = (grad_queries, grad_keys, grad_values)

    def target(step):
        dx, dy, dc = step
        to_chip = lax.rem(chip_y + dy, 4) * 4 + lax.rem(chip_x + dx, 4)
        return to_chip, lax.rem(core + dc, 2)

    def head_columns(of_chip):
        return pl.ds(pl.multiple_of(of_chip * HEAD_DIM, HEAD_DIM), HEAD_DIM)

    def tile_rows(device):
        return pl.ds(pl.multiple_of(device * TILE, TILE), TILE)

    def block_rows(n):
        return n // 2, pl.ds(pl.multiple_of(lax.rem(n, 2) * SUB, SUB), SUB)

    barrier = pltpu.get_barrier_semaphore()

    def greet(i, carry):
        pl.semaphore_signal(
            barrier, inc=1, device_id={"seq": lax.rem(me + i, 32)}, device_id_type=MESH
        )
        return carry

    lax.fori_loop(1, 32, greet, 0)

    def send_in(piece):
        for a, source in enumerate(sources):
            pltpu.make_async_copy(
                source.at[pl.ds(first_round(core, piece), PIECE), :, head_columns(chip)],
                held.at[a, pl.ds(first_slot(core, piece), PIECE), tile_rows(me), :],
                in_came.at[piece],
            ).start()
            for step in PEERS:
                to_chip, to_core = target(step)
                pltpu.make_async_remote_copy(
                    source.at[pl.ds(first_round(to_core, piece), PIECE), :, head_columns(to_chip)],
                    held.at[a, pl.ds(first_slot(to_core, piece), PIECE), tile_rows(me), :],
                    in_sent,
                    in_came.at[piece],
                    device_id={"seq": to_chip * 2 + to_core},
                    device_id_type=MESH,
                ).start()

    def send_out(piece):
        for a, result in enumerate(results):
            rounds = pl.ds(first_round(core, piece), PIECE)
            slots = pl.ds(first_slot(core, piece), PIECE)
            pltpu.make_async_copy(
                staged.at[a, slots, tile_rows(me), :],
                result.at[rounds, :, head_columns(chip)],
                out_came.at[a],
            ).start()
            for step in PEERS:
                to_chip, to_core = target(step)
                to = to_chip * 2 + to_core
                pltpu.make_async_remote_copy(
                    staged.at[a, slots, tile_rows(to), :],
                    result.at[rounds, :, head_columns(chip)],
                    out_sent,
                    out_came.at[a],
                    device_id={"seq": to},
                    device_id_type=MESH,
                ).start()

    before = lax.broadcasted_iota(jnp.int32, (HEAD_DIM, HEAD_DIM), 0) < lax.broadcasted_iota(
        jnp.int32, (HEAD_DIM, HEAD_DIM), 1
    )
    starts = jnp.dot(
        lens[...],
        jnp.where(before, 1.0, 0.0).astype(jnp.bfloat16),
        preferred_element_type=jnp.float32,
    )[0:1, :].astype(jnp.int32)
    ends = starts + lens[...].astype(jnp.float32)[0:1, :].astype(jnp.int32)

    def mark(n, carry):
        token = core * (HALF - 1) * 2 * SUB + n * SUB
        token = token + lax.broadcasted_iota(jnp.int32, (SUB, HEAD_DIM), 0)
        inside = (token >= starts) & (token < ends)
        place = block_rows(n)
        apart[*place] = jnp.where(inside, 0.0, FAR).astype(jnp.bfloat16)
        member[*place] = jnp.where(inside, 1.0, 0.0).astype(jnp.bfloat16)
        zeros = jnp.zeros((SUB, HEAD_DIM), jnp.float32)
        sum_keys[*place] = zeros
        sum_values[*place] = zeros
        return carry

    pl.semaphore_wait(barrier, 31)

    def send_piece(piece, carry):
        send_in(piece)
        return carry

    lax.fori_loop(0, PIECES, send_piece, 0)
    lax.fori_loop(0, SUBS, mark, 0)

    scale = 1.0 / math.sqrt(HEAD_DIM)
    log_scale = scale * math.log2(math.e)
    across = (((1,), (1,)), ((), ()))
    down = (((0,), (0,)), ((), ()))

    def attend(t):
        n = core * t + (1 - core) * (SUBS - 1 - t)
        first = jnp.clip(n - WINDOW // 2, 0, SUBS - WINDOW)
        here = block_rows(n)
        q_rows, c_rows = held[0, *here], held[3, *here]
        q_wide = jnp.concatenate([q_rows, apart[*here]], axis=1)
        places = [block_rows(first + i) for i in range(WINDOW)]
        scores = []
        for place in places:
            k_wide = jnp.concatenate([held[1, *place], member[*place]], axis=1)
            scores.append(
                lax.dot_general(k_wide, q_wide, across, preferred_element_type=jnp.float32)
            )
        top = functools.reduce(jnp.maximum, [jnp.max(s, axis=0, keepdims=True) for s in scores])
        top = top * log_scale
        weights = [jnp.exp2(s * log_scale - top) for s in scores]
        total = sum(jnp.sum(w, axis=0, keepdims=True) for w in weights)
        share = 1.0 / total
        probs = [w * share for w in weights]
        grad_probs = [
            lax.dot_general(held[2, *place], c_rows, across, preferred_element_type=jnp.float32)
            for place in places
        ]
        delta = sum(
            jnp.sum(p * g, axis=0, keepdims=True) for p, g in zip(probs, grad_probs, strict=True)
        )
        grad_q = jnp.zeros((SUB, HEAD_DIM), jnp.float32)
        for place, p, g in zip(places, probs, grad_probs, strict=True):
            grad_s = (p * (g - delta)).astype(jnp.bfloat16)
            sum_values[*place] += jnp.dot(
                p.astype(jnp.bfloat16), c_rows, preferred_element_type=jnp.float32
            )
            sum_keys[*place] += jnp.dot(grad_s, q_rows, preferred_element_type=jnp.float32)
            grad_q += lax.dot_general(
                grad_s, held[1, *place], down, preferred_element_type=jnp.float32
            )
        staged[0, *here] = (grad_q * scale).astype(jnp.bfloat16)

    def round_off(piece):
        def one(i, carry):
            place = block_rows(2 * first_slot(core, piece) + i)
            staged[1, *place] = (sum_keys[*place] * scale).astype(jnp.bfloat16)
            staged[2, *place] = sum_values[*place].astype(jnp.bfloat16)
            return carry

        lax.fori_loop(0, 2 * PIECE, one, 0)

    def beyond(side_sent, side_came):
        return pltpu.make_async_remote_copy(
            held.at[:, side_sent],
            held.at[:, side_came],
            halo_sent,
            halo_came,
            device_id={"seq": other},
            device_id_type=MESH,
        )

    per_piece = 2 * PIECE

    def step(t, carry):
        @pl.when((lax.rem(t, per_piece) == 0) & (t < PIECES * per_piece))
        def _():
            piece = t // per_piece
            arrived = held.at[:, pl.ds(first_slot(core, piece), PIECE)]
            pltpu.make_async_copy(arrived, arrived, in_came.at[piece]).wait()

        @pl.when(t == 0)
        def _():
            halo = beyond(core + (1 - core) * (HALF - 1), (1 - core) * 0 + core * HALF)
            halo.start()
            halo.wait()

        attend(t)
        last = t == SUBS - 1

        @pl.when(((lax.rem(t, per_piece) == per_piece - 1) & (t >= 2 * per_piece - 1)) | last)
        def _():
            piece = jnp.where(last, PIECES - 1, (t - (per_piece - 1)) // per_piece - 1)
            round_off(piece)
            send_out(piece)

        return carry

    lax.fori_loop(0, SUBS, step, 0)

    for a, result in enumerate(results):
        pltpu.make_async_copy(result, result, out_came.at[a]).wait()
    most = pl.ds(0, 31 * TILE)
    left = held.at[:, pl.ds(0, HALF), most, :]
    pltpu.make_async_copy(left, left, in_sent).wait()
    left = staged.at[:, pl.ds(0, HALF), most, :]
    pltpu.make_async_copy(left, left, out_sent).wait()


def per_device(queries, keys, values, cotangent, lengths):
    lens = jnp.pad(lengths, (0, HEAD_DIM - lengths.shape[0])).astype(jnp.bfloat16)
    lens = jnp.broadcast_to(lens[None], (TILE, HEAD_DIM))
    anywhere = pl.BlockSpec(memory_space=pl.ANY)
    block = (SLOTS, 2 * SUB, HEAD_DIM)
    return pl.pallas_call(
        kernel,
        out_shape=[jax.ShapeDtypeStruct(queries.shape, jnp.bfloat16)] * 3,
        in_specs=[anywhere] * 4 + [pl.BlockSpec(memory_space=pltpu.VMEM)],
        out_specs=[anywhere] * 3,
        scratch_shapes=[
            pltpu.VMEM((4, *block), jnp.bfloat16),
            pltpu.VMEM(block, jnp.bfloat16),
            pltpu.VMEM(block, jnp.bfloat16),
            pltpu.VMEM(block, jnp.float32),
            pltpu.VMEM(block, jnp.float32),
            pltpu.VMEM((3, *block), jnp.bfloat16),
            pltpu.SemaphoreType.DMA,
            pltpu.SemaphoreType.DMA((PIECES,)),
            pltpu.SemaphoreType.DMA,
            pltpu.SemaphoreType.DMA,
            pltpu.SemaphoreType.DMA,
            pltpu.SemaphoreType.DMA((3,)),
        ],
        compiler_params=pltpu.CompilerParams(
            collective_id=0, has_side_effects=True, vmem_limit_bytes=56 * 2**20
        ),
        name="attention_grads",
    )(queries, keys, values, cotangent, lens)


def solution(mesh):
    rows = P(None, ("grp", "seq"), None)
    return jax.shard_map(
        per_device,
        mesh=mesh,
        in_specs=(rows, rows, rows, rows, P("grp")),
        out_specs=(rows, rows, rows),
        check_vma=False,
    )
```

time: 1060 us -> 157 us (0.15); the launches traced: 1040 us -> 157 us
  other arithmetic: 391 us -> 0.66 us
  waiting for transfers between devices: 353 us -> 0 us
  local copies, waits for them, and re-layouts: 203 us -> 7.07 us
  Pallas kernels: 0 us -> 148 us
  matrix products: 61.6 us -> 0 us
  starting transfers between devices: 32.3 us -> 0 us
    all_to_all x3 -> x0, waiting for transfers between devices: 353 us -> none  [the longest x1 202 us: per_device(): lax.all_to_all(outgoing, 'seq', split_axis=1, concat_axis=1, tiled=True)]
    reduce_sum x180 -> x0, other arithmetic: 164 us -> none  [the longest x98 91.7 us: lookup(): return jnp.sum(jnp.where(hits, table, 0), axis=-1)]
    pallas_call x0 -> x1, Pallas kernels: none -> 148 us  [per_device(): pl.pallas_call(kernel, out_shape=[jax.ShapeDtypeStruct(queries.shape, jnp...]
    select_n x85 -> x0, other arithmetic: 111 us -> none  [the longest x48 91.3 us: place(): slot_of = jnp.where(is_doc, slot_now, slot_of)]
    dynamic_slice x38 -> x0, local copies, waits for them, and re-layouts: 73.7 us -> none  [the longest x6 39.3 us: owner_work(): lax.map(lambda member: slot_grads(member[0], member[1]), (rows_in, valid_...]
    dot_general x192 -> x0, matrix products: 61.6 us -> none  [the longest x32 12.6 us: head_grads(): jnp.dot(query_rows, key_rows.T, preferred_element_type=jnp.float32)]
    dynamic_update_slice x68 -> x0, local copies, waits for them, and re-layouts: 61.2 us -> none  [the longest x4 30.7 us: owner_work(): lax.map(lambda member: slot_grads(member[0], member[1]), (rows_in, valid_...]
    add x50 -> x0, other arithmetic: 60.3 us -> none  [the longest x48 60.3 us: place(): owner_loads = owner_loads + jnp.where(picked, lookup(doc_cost, current), 0)]
  transfers between devices with their start and end apart: 3 -> 0, of which waited for: 2 -> 0; matrix products, arithmetic and copies ran while one was open for 3% -> 0% of each run, Pallas kernels for 0% -> 0%
where the time goes in v1:
time: 157 us
  Pallas kernels  148 us (94%)
  local copies, waits for them, and re-layouts  7.07 us (5%)
    pallas_call x1, Pallas kernels, per_device(): pl.pallas_call(kernel, out_shape=[jax.ShapeDtypeStruct(queries.shape, jnp...  148 us
    unnamed x7, local copies, waits for them, and re-layouts  6.46 us

profile of v1, /device:TPU:1, one launch (start us, length us, event | category | flops | bytes accessed | tf_op | source)
XLA Modules:
  0.0 156.7 jit_solution(15343132233449180209)
XLA Ops:
  0.6 0.7 convert.4
  1.3 0.6 broadcast_in_dim.2.lens
  1.9 148.3 %attention_grads.1 = (bf16[28,16,2048]{2,1,0:T(8,128)(2,1)}, bf16[28,16,2048]{2,1,0:T(8,128)(2,1)}, bf16[28,16,2048]{2,1,0:T(8,128)(2,1)}) custom-call(bf16[28,16,2048]{2,1,0:T(8,128)(2,1)} %queries.1, bf16[28,16,2048]{2,1,0:T(8,128)(2,1)} %keys.1, bf16[28,16,2048]{2,1,0:T(8,128)(2,1)} %values.1, bf16[28,16,2048]{2,1,0:T(8,128)(2,1)} %cotangent.1, ...), custom_call_target="tpu_custom_call" | custom-call | tf_op jit(solution)/shard_map/attention_grads/pallas_call | solution.py:248
  150.2 0.0 copy-start.1
  150.2 3.1 %copy.11 = bf16[28,16,2048]{2,1,0:T(8,128)(2,1)} copy(bf16[28,16,2048]{2,1,0:T(8,128)(2,1)} %get-tuple-element.6) | data formatting | bytes 3670016
  153.3 0.0 copy-done.1
  153.3 0.0 copy-start
  153.3 1.2 copy.12
  154.5 0.9 copy-done
  155.4 1.2 copy.13
  (1 shorter events, 0.0 us)
Async XLA Ops:
  150.2 3.1 %copy-start.1 = (bf16[28,16,2048]{2,1,0:T(8,128)(2,1)S(1)}, bf16[28,16,2048]{2,1,0:T(8,128)(2,1)}, u32[]{:S(2)}) copy-start(bf16[28,16,2048]{2,1,0:T(8,128)(2,1)} %get-tuple-element.7) | copy-start | bytes 5505028
  153.3 2.2 %copy-start = (bf16[28,16,2048]{2,1,0:T(8,128)(2,1)S(1)}, bf16[28,16,2048]{2,1,0:T(8,128)(2,1)}, u32[]{:S(2)}) copy-start(bf16[28,16,2048]{2,1,0:T(8,128)(2,1)} %get-tuple-element.8) | copy-start | bytes 5505028

commit v2 on v1

--- a/solution.py
+++ b/solution.py
@@ -23,6 +23,7 @@
 HALF = PIECE * PIECES
 SLOTS = HALF + 1
 SUBS = 2 * SLOTS
+PART = 7
 WINDOW = 5
 
 
@@ -240,12 +241,35 @@
     pltpu.make_async_copy(left, left, out_sent).wait()
 
 
+def write_out(*refs):
+    sources, results, (held, came, sent) = refs[:3], refs[3:6], refs[6:]
+
+    def part(ref, i):
+        return ref.at[pl.ds(PART * i, PART)]
+
+    def fetch(a, i):
+        return pltpu.make_async_copy(part(sources[a], i), part(held.at[a], i), came.at[a, i])
+
+    def store(a, i):
+        return pltpu.make_async_copy(part(held.at[a], i), part(results[a], i), sent.at[a, i])
+
+    order = [(a, i) for i in range(results[0].shape[0] // PART) for a in range(3)]
+    for place in order:
+        fetch(*place).start()
+    for place in order:
+        fetch(*place).wait()
+        store(*place).start()
+    for place in order:
+        store(*place).wait()
+
+
 def per_device(queries, keys, values, cotangent, lengths):
     lens = jnp.pad(lengths, (0, HEAD_DIM - lengths.shape[0])).astype(jnp.bfloat16)
     lens = jnp.broadcast_to(lens[None], (TILE, HEAD_DIM))
     anywhere = pl.BlockSpec(memory_space=pl.ANY)
     block = (SLOTS, 2 * SUB, HEAD_DIM)
-    return pl.pallas_call(
+    parts = queries.shape[0] // PART
+    grads = pl.pallas_call(
         kernel,
         out_shape=[jax.ShapeDtypeStruct(queries.shape, jnp.bfloat16)] * 3,
         in_specs=[anywhere] * 4 + [pl.BlockSpec(memory_space=pltpu.VMEM)],
@@ -269,6 +293,19 @@
         ),
         name="attention_grads",
     )(queries, keys, values, cotangent, lens)
+    return pl.pallas_call(
+        write_out,
+        out_shape=[jax.ShapeDtypeStruct(queries.shape, jnp.bfloat16)] * 3,
+        in_specs=[anywhere] * 3,
+        out_specs=[anywhere] * 3,
+        scratch_shapes=[
+            pltpu.VMEM((3, *queries.shape), jnp.bfloat16),
+            pltpu.SemaphoreType.DMA((3, parts)),
+            pltpu.SemaphoreType.DMA((3, parts)),
+        ],
+        compiler_params=pltpu.CompilerParams(vmem_limit_bytes=56 * 2**20),
+        name="write_out",
+    )(*grads)
 
 
 def solution(mesh):

time: 157 us -> 155 us (0.987)
  local copies, waits for them, and re-layouts: 7.07 us -> 0.6 us
  Pallas kernels: 148 us -> 153 us
    unnamed x7 -> x0, local copies, waits for them, and re-layouts: 6.46 us -> none
    pallas_call x0 -> x1, Pallas kernels: none -> 5.03 us  [per_device(): pl.pallas_call(write_out, out_shape=[jax.ShapeDtypeStruct(queries.shape,...]
where the time goes in v2:
time: 155 us
  Pallas kernels  153 us (99%)
    pallas_call x1, Pallas kernels, per_device(): pl.pallas_call(kernel, out_shape=[jax.ShapeDtypeStruct(queries.shape, jnp...  148 us
    pallas_call x1, Pallas kernels, per_device(): pl.pallas_call(write_out, out_shape=[jax.ShapeDtypeStruct(queries.shape,...  5.03 us

profile of v2, /device:TPU:1, one launch (start us, length us, event | category | flops | bytes accessed | tf_op | source)
XLA Modules:
  0.0 155.2 jit_solution(14098032604418208460)
XLA Ops:
  0.6 0.7 convert.4
  1.3 0.6 broadcast_in_dim.2.lens
  1.9 148.3 %attention_grads.1 = (bf16[28,16,2048]{2,1,0:T(8,128)(2,1)}, bf16[28,16,2048]{2,1,0:T(8,128)(2,1)}, bf16[28,16,2048]{2,1,0:T(8,128)(2,1)}) custom-call(bf16[28,16,2048]{2,1,0:T(8,128)(2,1)} %queries.1, bf16[28,16,2048]{2,1,0:T(8,128)(2,1)} %keys.1, bf16[28,16,2048]{2,1,0:T(8,128)(2,1)} %values.1, bf16[28,16,2048]{2,1,0:T(8,128)(2,1)} %cotangent.1, ...), custom_call_target="tpu_custom_call" | custom-call | tf_op jit(solution)/shard_map/attention_grads/pallas_call | solution.py:272
  150.2 5.0 %write_out.1 = (bf16[28,16,2048]{2,1,0:T(8,128)(2,1)}, bf16[28,16,2048]{2,1,0:T(8,128)(2,1)}, bf16[28,16,2048]{2,1,0:T(8,128)(2,1)}) custom-call(bf16[28,16,2048]{2,1,0:T(8,128)(2,1)} %get-tuple-element.6.refs_0_, bf16[28,16,2048]{2,1,0:T(8,128)(2,1)} %get-tuple-element.7.refs_1_, bf16[28,16,2048]{2,1,0:T(8,128)(2,1)} %get-tuple-element.8.refs_2_), custom_call_target="tpu_custom_call" | custom-call | tf_op jit(solution)/shard_map/write_out/pallas_call | solution.py:296
  (1 shorter events, 0.0 us)

commit v3 on v2

--- a/solution.py
+++ b/solution.py
@@ -111,15 +111,16 @@
                     device_id_type=MESH,
                 ).start()
 
-    before = lax.broadcasted_iota(jnp.int32, (HEAD_DIM, HEAD_DIM), 0) < lax.broadcasted_iota(
-        jnp.int32, (HEAD_DIM, HEAD_DIM), 1
-    )
-    starts = jnp.dot(
-        lens[...],
-        jnp.where(before, 1.0, 0.0).astype(jnp.bfloat16),
-        preferred_element_type=jnp.float32,
-    )[0:1, :].astype(jnp.int32)
-    ends = starts + lens[...].astype(jnp.float32)[0:1, :].astype(jnp.int32)
+    table = (lens.shape[1], HEAD_DIM)
+    row = lax.broadcasted_iota(jnp.int32, table, 0)
+    column = lax.broadcasted_iota(jnp.int32, table, 1)
+    sizes = jnp.broadcast_to(lens[...].astype(jnp.float32), (TILE, table[0])).astype(jnp.bfloat16)
+
+    def total(chosen):
+        chosen = jnp.where(chosen, 1.0, 0.0).astype(jnp.bfloat16)
+        return jnp.dot(sizes, chosen, preferred_element_type=jnp.float32)[0:1, :].astype(jnp.int32)
+
+    starts, ends = total(row < column), total(row <= column)
 
     def mark(n, carry):
         token = core * (HALF - 1) * 2 * SUB + n * SUB
@@ -264,8 +265,6 @@
 
 
 def per_device(queries, keys, values, cotangent, lengths):
-    lens = jnp.pad(lengths, (0, HEAD_DIM - lengths.shape[0])).astype(jnp.bfloat16)
-    lens = jnp.broadcast_to(lens[None], (TILE, HEAD_DIM))
     anywhere = pl.BlockSpec(memory_space=pl.ANY)
     block = (SLOTS, 2 * SUB, HEAD_DIM)
     parts = queries.shape[0] // PART
@@ -292,7 +291,7 @@
             collective_id=0, has_side_effects=True, vmem_limit_bytes=56 * 2**20
         ),
         name="attention_grads",
-    )(queries, keys, values, cotangent, lens)
+    )(queries, keys, values, cotangent, lengths.reshape(1, -1))
     return pl.pallas_call(
         write_out,
         out_shape=[jax.ShapeDtypeStruct(queries.shape, jnp.bfloat16)] * 3,

time: 155 us -> 154 us (level)
  no operation moved by 1% of the time
where the time goes in v3:
time: 154 us
  Pallas kernels  153 us (99%)
    pallas_call x1, Pallas kernels, per_device(): pl.pallas_call(kernel, out_shape=[jax.ShapeDtypeStruct(queries.shape, jnp...  148 us
    pallas_call x1, Pallas kernels, per_device(): pl.pallas_call(write_out, out_shape=[jax.ShapeDtypeStruct(queries.shape,...  5.03 us

profile of v3, /device:TPU:1, one launch (start us, length us, event | category | flops | bytes accessed | tf_op | source)
XLA Modules:
  0.0 153.9 jit_solution(17990292062648394318)
XLA Ops:
  0.6 148.3 %attention_grads.1 = (bf16[28,16,2048]{2,1,0:T(8,128)(2,1)}, bf16[28,16,2048]{2,1,0:T(8,128)(2,1)}, bf16[28,16,2048]{2,1,0:T(8,128)(2,1)}) custom-call(bf16[28,16,2048]{2,1,0:T(8,128)(2,1)} %queries.1, bf16[28,16,2048]{2,1,0:T(8,128)(2,1)} %keys.1, bf16[28,16,2048]{2,1,0:T(8,128)(2,1)} %values.1, bf16[28,16,2048]{2,1,0:T(8,128)(2,1)} %cotangent.1, ...), custom_call_target="tpu_custom_call" | custom-call | tf_op jit(solution)/shard_map/attention_grads/pallas_call | solution.py:271
  148.9 5.0 %write_out.1 = (bf16[28,16,2048]{2,1,0:T(8,128)(2,1)}, bf16[28,16,2048]{2,1,0:T(8,128)(2,1)}, bf16[28,16,2048]{2,1,0:T(8,128)(2,1)}) custom-call(bf16[28,16,2048]{2,1,0:T(8,128)(2,1)} %get-tuple-element.6.refs_0_, bf16[28,16,2048]{2,1,0:T(8,128)(2,1)} %get-tuple-element.7.refs_1_, bf16[28,16,2048]{2,1,0:T(8,128)(2,1)} %get-tuple-element.8.refs_2_), custom_call_target="tpu_custom_call" | custom-call | tf_op jit(solution)/shard_map/write_out/pallas_call | solution.py:295
